TPU v7x, 512 devices: a whole 4x4x16 slice. The times are simulated.
512 devices in a mesh: rows: 32 (over z_lo, x), cols: 16 (over y, z_hi, core).
Axes of the slice: x: 4, y: 4, z: 16 (z_hi: 2, z_lo: 8; z = z_hi * 8 + z_lo), core: 2. Of those that a mesh axis runs over, the one named last changes fastest.
Arguments:
- left_feat: bfloat16 [320, 32, 2048], P(None, 'rows', 'cols'), may hold values from -6 to 6
- right_feat: bfloat16 [320, 32, 2048], P(None, 'rows', 'cols'), may hold values from -6 to 6
- grad_out: bfloat16 [32, 48, 32, 2048], P(None, None, 'rows', 'cols'), may hold values from -6 to 6
- conv_weight: bfloat16 [32, 40, 3, 3, 3], replicated, may hold values from -0.21875 to 0.21875
Outputs:
- grad_left: bfloat16 [320, 32, 2048], P(None, 'rows', 'cols')
- grad_right: bfloat16 [320, 32, 2048], P(None, 'rows', 'cols')
- grad_weight: float32 [32, 40, 3, 3, 3], replicated
All inputs are finite; a program needn't handle non-finite values.
Results may differ from a plain program's by a relative error of at most 0.0029.
Values may be sent and summed in bfloat16 or wider, within the bound.
A program may use at most 64 MiB of HBM per device.

v0:
```python
import math

import jax
import jax.numpy as jnp
from jax import lax
from jax.sharding import PartitionSpec as P


def from_behind(shard, axis, by):
    count = lax.axis_size(axis)
    pairs = [(i, i + by) for i in range(count) if 0 <= i + by < count]
    return lax.ppermute(shard, axis, pairs)


def padded_2(shard, sides, width):
    for axis, dim in sides:
        count, length = (lax.axis_size(axis), shard.shape[dim])
        up = [(i, (i + 1) % count) for i in range(count - 1)]
        down = [(j, i) for i, j in up]
        last = lax.slice_in_dim(shard, length - width, length, axis=dim)
        initial = lax.slice_in_dim(shard, 0, width, axis=dim)
        before = lax.ppermute(last, axis, up)
        after = lax.ppermute(initial, axis, down)
        shard = jnp.concatenate([before, shard, after], axis=dim)
    return shard


def correlate(left_band, right_ext, levels, groups):
    channels, band_rows, tile_width = left_band.shape
    group_size = channels // groups
    left_wide = left_band.astype(jnp.float32)
    start_volume = jnp.zeros((groups, levels, band_rows, tile_width), jnp.float32)

    def correlate_one_level(level, volume):
        offset = (levels - 1 - level).astype(jnp.int32)
        shifted = lax.dynamic_slice_in_dim(right_ext, offset, tile_width, 2).astype(jnp.float32)
        product = (left_wide * shifted).reshape(groups, group_size, band_rows, tile_width)
        slab = jnp.sum(product, axis=1) * (1.0 / group_size)
        return lax.dynamic_update_slice_in_dim(volume, slab[:, None], level, 1)

    return lax.fori_loop(0, levels, correlate_one_level, start_volume)


def feature_grads(grad_volume, left_band, right_ext, levels, groups):
    channels, band_rows, tile_width = left_band.shape
    group_size = channels // groups
    left_wide = left_band.astype(jnp.float32).reshape(groups, group_size, band_rows, tile_width)
    start_left = jnp.zeros((groups, group_size, band_rows, tile_width), jnp.float32)
    start_ext = jnp.zeros((channels, band_rows, tile_width + levels - 1), jnp.float32)

    def feature_one_level(level, carry):
        grad_left, grad_ext = carry
        offset = (levels - 1 - level).astype(jnp.int32)
        shifted = lax.dynamic_slice_in_dim(right_ext, offset, tile_width, 2).astype(jnp.float32)
        slab = lax.dynamic_slice_in_dim(grad_volume, level, 1, 1)
        grad_left = grad_left + slab * shifted.reshape(groups, group_size, band_rows, tile_width)
        spread = (slab * left_wide).reshape(channels, band_rows, tile_width)
        current = lax.dynamic_slice_in_dim(grad_ext, offset, tile_width, 2)
        grad_ext = lax.dynamic_update_slice_in_dim(grad_ext, current + spread, offset, 2)
        return (grad_left, grad_ext)

    grad_left, grad_ext = lax.fori_loop(0, levels, feature_one_level, (start_left, start_ext))
    scale = 1.0 / group_size
    return (grad_left.reshape(channels, band_rows, tile_width) * scale, grad_ext * scale)


def kernel_terms(volume, padded, levels, band_rows, tile_width):
    terms = []
    for along_d in range(3):
        for along_h in range(3):
            for along_w in range(3):
                window_cut = padded[
                    :,
                    2 - along_d : 2 - along_d + levels,
                    2 - along_h : 2 - along_h + band_rows,
                    2 - along_w : 2 - along_w + tile_width,
                ]
                terms.append(
                    lax.dot_general(
                        window_cut,
                        volume,
                        (((1, 2, 3), (1, 2, 3)), ((), ())),
                        preferred_element_type=jnp.float32,
                    )
                )
    stacked = jnp.stack(terms, axis=-1)
    return stacked.reshape(stacked.shape[0], stacked.shape[1], 3, 3, 3)


def shards(left_feat, right_feat, grad_out, conv_weight):
    channels, band_rows, tile_width = left_feat.shape
    levels = grad_out.shape[1]
    groups = conv_weight.shape[1]
    margin_cols = levels - 1
    shifted_tile = from_behind(right_feat, "cols", 1)
    border = shifted_tile[:, :, tile_width - margin_cols :]
    right_ext = jnp.concatenate([border, right_feat], axis=2)
    volume = correlate(left_feat, right_ext, levels, groups).astype(jnp.bfloat16)
    padded = padded_2(grad_out, (("rows", 2), ("cols", 3)), 1)
    padded = jnp.pad(padded, ((0, 0), (1, 1), (0, 0), (0, 0)))
    flipped = jnp.transpose(jnp.flip(conv_weight, (2, 3, 4)), (1, 0, 2, 3, 4))
    layout = ("NCDHW", "OIDHW", "NCDHW")
    kernel_local = kernel_terms(volume, padded, levels, band_rows, tile_width)
    summed = lax.psum(kernel_local, ("rows", "cols"))
    grad_volume = lax.conv_general_dilated(
        padded[None],
        flipped,
        (1, 1, 1),
        "VALID",
        dimension_numbers=layout,
        preferred_element_type=jnp.float32,
    )[0]
    cells = levels * band_rows * lax.axis_size("rows") * tile_width * lax.axis_size("cols")
    grad_weight = summed * (1.0 / math.sqrt(cells))
    grad_left, grad_ext = feature_grads(grad_volume, left_feat, right_ext, levels, groups)
    own_part = grad_ext[:, :, margin_cols:]
    spill = grad_ext[:, :, :margin_cols]
    spill_tile = jnp.pad(spill, ((0, 0), (0, 0), (tile_width - margin_cols, 0)))
    arrived = from_behind(spill_tile, "cols", -1)
    grad_right = own_part + arrived
    return (grad_left.astype(jnp.bfloat16), grad_right.astype(jnp.bfloat16), grad_weight)


def solution(mesh):
    placed = (P(None, "rows", "cols"), P(None, "rows", "cols"), P(None, None, "rows", "cols"), P())
    return jax.shard_map(
        shards,
        mesh=mesh,
        in_specs=placed,
        out_specs=(P(None, "rows", "cols"), P(None, "rows", "cols"), P()),
        check_vma=False,
    )
```

profile of v0, /device:TPU:1, one launch (start us, length us, event | category | flops | bytes accessed | tf_op | source)
XLA Modules:
  0.0 599.6 jit_solution(4668678989046985764)
XLA Ops:
  8.4 4.0 collective-permute-start
  13.7 16.3 %collective-permute-start.4 = (bf16[320,1,128]{2,0,1:T(8,128)(2,1)}, bf16[320,1,128]{2,0,1:T(8,128)(2,1)S(1)}, u32[]{:S(2)}, u32[]{:S(2)}) collective-permute-start(bf16[320,1,128]{2,0,1:T(8,128)(2,1)} %param.9), channel_id=1, source_target_pairs={{0,1},{1,2},{2,3},{3,4},{4,5},{5,6},{6,7},{7,8},{8,9},{9,10},{10,1... | collective-permute-start | bytes 245768 | tf_op jit(solution)/shard_map/ppermute | solution.py:12
  32.8 46.2 %while.33 = (s32[]{:T(128)}, f32[40,48,1,128]{3,2,1,0:T(1,128)}, bf16[320,1,175]{2,0,1:T(8,128)(2,1)S(1)}, f32[320,1,128]{2,1,0:T(1,128)S(1)}, s32[]{:T(128)}, /*index=5*/s32[]{:T(128)}, s32[]{:T(128)}, s32[]{:T(128)}) while((s32[]{:T(128)}, f32[40,48,1,128]{3,2,1,0:T(1,128)}, bf16[320,1,175]{2,0,1:T(8,128)(2,1)S(1)}, ...), condition=%wide.region_4.5_spmd, body=%wide.region_2.4_spmd.sunk | while | flops 122886 | bytes 840327 | solution.py:41
  81.3 1.6 fusion.78
  82.9 2.5 copy.85
  85.4 13.0 %collective-permute-start.2 = (bf16[32,48,3,1]{1,0,3,2:T(8,128)(2,1)S(1)}, bf16[32,48,3,1]{1,0,3,2:T(8,128)(2,1)S(1)}, u32[]{:S(2)}, u32[]{:S(2)}) collective-permute-start(bf16[32,48,3,1]{1,0,3,2:T(8,128)(2,1)S(1)} %copy.85), channel_id=1, source_target_pairs={{0,1},{1,2},{2,3},{3,4},{4,5},{5,6},{6,7},{7,8},{8,9},{9,10},{10,1... | collective-permute-start | bytes 27656 | tf_op jit(solution)/shard_map/ppermute | solution.py:22
  99.8 1.9 collective-permute-start.3
  103.0 1.9 copy.87
  104.9 8.7 %collective-permute-done.3 = bf16[32,48,3,1]{1,0,3,2:T(8,128)(2,1)S(1)} collective-permute-done((bf16[32,48,3,1]{1,0,3,2:T(8,128)(2,1)S(1)}, bf16[32,48,3,1]{1,0,3,2:T(8,128)(2,1)S(1)}, u32[]{:S(2)}, u32[]{:S(2)}) %collective-permute-start.3) | collective-permute-done | bytes 9248 | tf_op jit(solution)/shard_map/ppermute | solution.py:23
  113.6 2.9 copy.88
  116.5 2.8 fusion.16
  119.3 2.7 fusion.80
  132.3 5.7 copy.134
  138.0 4.3 pad.10.clone
  142.4 7.2 %copy.91 = bf16[32,50,3,1,8,17]{0,4,5,2,1,3:T(8,128)(2,1)} copy(bf16[32,50,3,1,8,17]{1,0,5,4,2,3:T(8,128)(2,1)} %bitcast.194) | data formatting | bytes 2611200 | tf_op jit(solution)/shard_map/conv_general_dilated | solution.py:105
  150.9 10.0 %fusion.17 = f32[48,1,8,17,40]{4,2,3,1,0:T(8,128)} fusion(bf16[32,40,3,3,3]{1,0,4,3,2:T(8,128)(2,1)S(1)} %copy-done, bf16[32,50,3,1,7,2]{0,4,5,2,1,3:T(8,128)(2,1)S(1)} %slice.141, bf16[32,50,3,1,8,17]{0,4,5,2,1,3:T(8,128)(2,1)} %copy.91, pred[8,17]{0,1:T(8,128)(4,1)S(1)} %copy-done.11), kind=kOutput, calls=%fused_computation.30 | convolution fusion | flops 455854080 | bytes 2553736 | tf_op jit(solution)/shard_map/conv_general_dilated | solution.py:105
  160.9 3.5 copy.92
  164.5 1.7 slice_bitcast_fusion
  166.2 2.5 copy.94
  168.7 109.2 %while.34 = (s32[]{:T(128)}, f32[40,8,1,128]{3,2,1,0:T(1,128)S(1)}, f32[320,1,175]{2,0,1:T(8,128)S(1)}, f32[40,48,1,128]{3,0,2,1:T(8,128)S(1)}, bf16[320,1,175]{...) while((s32[]{:T(128)}, f32[40,8,1,128]{3,2,1,0:T(1,128)S(1)}, ...), condition=%wide.region_1.2_spmd.clone, body=%wide.region_0.1_spmd.clone.sunk | while | flops 245767 | bytes 2293933 | solution.py:62
  168.9 1.6 dynamic_update_slice.25
  171.2 1.6 dynamic_update_slice.25
  173.4 1.6 dynamic_update_slice.25
  175.7 1.6 dynamic_update_slice.25
  178.0 1.6 dynamic_update_slice.25
  180.3 1.6 dynamic_update_slice.25
  182.6 1.6 dynamic_update_slice.25
  184.8 1.6 dynamic_update_slice.25
  187.1 1.6 dynamic_update_slice.25
  189.4 1.6 dynamic_update_slice.25
  191.7 1.6 dynamic_update_slice.25
  194.0 1.6 dynamic_update_slice.25
  196.2 1.6 dynamic_update_slice.25
  198.5 1.6 dynamic_update_slice.25
  200.8 1.6 dynamic_update_slice.25
  203.1 1.6 dynamic_update_slice.25
  205.4 1.6 dynamic_update_slice.25
  207.6 1.6 dynamic_update_slice.25
  209.9 1.6 dynamic_update_slice.25
  212.2 1.6 dynamic_update_slice.25
  214.5 1.6 dynamic_update_slice.25
  216.8 1.6 dynamic_update_slice.25
  219.0 1.6 dynamic_update_slice.25
  221.3 1.6 dynamic_update_slice.25
  223.6 1.6 dynamic_update_slice.25
  225.9 1.6 dynamic_update_slice.25
  228.2 1.6 dynamic_update_slice.25
  230.4 1.6 dynamic_update_slice.25
  232.7 1.6 dynamic_update_slice.25
  235.0 1.6 dynamic_update_slice.25
  237.3 1.6 dynamic_update_slice.25
  239.6 1.6 dynamic_update_slice.25
  241.8 1.6 dynamic_update_slice.25
  244.1 1.6 dynamic_update_slice.25
  246.4 1.6 dynamic_update_slice.25
  248.7 1.6 dynamic_update_slice.25
  251.0 1.6 dynamic_update_slice.25
  253.2 1.6 dynamic_update_slice.25
  255.5 1.6 dynamic_update_slice.25
  257.8 1.6 dynamic_update_slice.25
  260.1 1.6 dynamic_update_slice.25
  278.0 1.9 collective-permute-start.5
  280.6 309.6 %all-reduce.4.cloned.1.call-done = f32[32,40,3,3,3]{1,0,4,3,2:T(8,128)} async-done(((f32[32,40,3,3,3]{1,0,4,3,2:T(8,128)}), f32[32,40,3,3,3]{1,0,4,3,2:T(8,128)}) %all-reduce.4.cloned.1.call-update) | async-done | bytes 138256 | tf_op jit(solution)/shard_map/psum | solution.py:104
  590.2 1.8 broadcast_multiply_fusion.1
  (612 shorter events, 109.0 us)
Async XLA Ops:
  7.2 143.7 %copy-start = (bf16[32,40,3,3,3]{1,0,4,3,2:T(8,128)(2,1)S(1)}, bf16[32,40,3,3,3]{1,0,4,3,2:T(8,128)(2,1)}, u32[]{:S(2)}) copy-start(bf16[32,40,3,3,3]{1,0,4,3,2:T(8,128)(2,1)} %param.11) | copy-start | bytes 207364
  7.2 583.0 %all-reduce.4.cloned.1.call-start = ((), (), s32[]{:S(2)}) async-start(), calls=%async_computation | async-start | bytes 884736 | tf_op jit(solution)/shard_map/psum | solution.py:104
  8.4 71.4 %collective-permute-start = (bf16[32,48,1,128]{3,0,1,2:T(8,128)(2,1)S(1)}, bf16[32,48,1,128]{3,0,1,2:T(8,128)(2,1)S(1)}, u32[]{:S(2)}, u32[]{:S(2)}) collective-permute-start(bf16[32,48,1,128]{3,0,1,2:T(8,128)(2,1)S(1)} %copy.82), channel_id=1, source_target_pairs={{0,16},{16,32},{32,48},{48,64},{64,80},{80,96},{96,112},{112,128},... | collective-permute-start | bytes 1179656 | tf_op jit(solution)/shard_map/ppermute | solution.py:22
  12.4 67.6 %collective-permute-start.1 = (bf16[32,48,1,128]{3,0,1,2:T(8,128)(2,1)S(1)}, bf16[32,48,1,128]{3,0,1,2:T(8,128)(2,1)S(1)}, u32[]{:S(2)}, u32[]{:S(2)}) collective-permute-start(bf16[32,48,1,128]{3,0,1,2:T(8,128)(2,1)S(1)} %copy.82), channel_id=1, source_target_pairs={{16,0},{32,16},{48,32},{64,48},{80,64},{96,80},{112,96},{128,112},... | collective-permute-start | bytes 1179656 | tf_op jit(solution)/shard_map/ppermute | solution.py:23
  13.7 18.1 %collective-permute-start.4 = (bf16[320,1,128]{2,0,1:T(8,128)(2,1)}, bf16[320,1,128]{2,0,1:T(8,128)(2,1)S(1)}, u32[]{:S(2)}, u32[]{:S(2)}) collective-permute-start(bf16[320,1,128]{2,0,1:T(8,128)(2,1)} %param.9), channel_id=1, source_target_pairs={{0,1},{1,2},{2,3},{3,4},{4,5},{5,6},{6,7},{7,8},{8,9},{9,10},{10,1... | collective-permute-start | bytes 245768 | tf_op jit(solution)/shard_map/ppermute | solution.py:12
  32.8 47.0 %copy-start.4 = (bf16[32,48,1,128]{3,1,2,0:T(8,128)(2,1)S(1)}, bf16[32,48,1,128]{3,1,2,0:T(8,128)(2,1)}, u32[]{:S(2)}) copy-start(bf16[32,48,1,128]{3,1,2,0:T(8,128)(2,1)} %param.10) | copy-start | bytes 1179652
  79.1 0.7 copy-start.2
  79.8 0.7 copy-start.7
  80.5 0.7 copy-start.9
  85.4 17.6 %collective-permute-start.2 = (bf16[32,48,3,1]{1,0,3,2:T(8,128)(2,1)S(1)}, bf16[32,48,3,1]{1,0,3,2:T(8,128)(2,1)S(1)}, u32[]{:S(2)}, u32[]{:S(2)}) collective-permute-start(bf16[32,48,3,1]{1,0,3,2:T(8,128)(2,1)S(1)} %copy.85), channel_id=1, source_target_pairs={{0,1},{1,2},{2,3},{3,4},{4,5},{5,6},{6,7},{7,8},{8,9},{9,10},{10,1... | collective-permute-start | bytes 27656 | tf_op jit(solution)/shard_map/ppermute | solution.py:22
  99.8 13.9 %collective-permute-start.3 = (bf16[32,48,3,1]{1,0,3,2:T(8,128)(2,1)S(1)}, bf16[32,48,3,1]{1,0,3,2:T(8,128)(2,1)S(1)}, u32[]{:S(2)}, u32[]{:S(2)}) collective-permute-start(bf16[32,48,3,1]{1,0,3,2:T(8,128)(2,1)S(1)} %copy.86), channel_id=1, source_target_pairs={{1,0},{2,1},{3,2},{4,3},{5,4},{6,5},{7,6},{8,7},{9,8},{10,9},{11,1... | collective-permute-start | bytes 27656 | tf_op jit(solution)/shard_map/ppermute | solution.py:23
  116.5 2.8 copy-start.1
  124.3 1.1 copy-start.10
  125.6 1.0 copy-start.5
  126.9 1.0 copy-start.8
  131.5 0.8 copy-start.6
  142.4 8.5 %copy-start.11 = (pred[8,17]{0,1:T(8,128)(4,1)S(1)}, pred[8,17]{0,1:T(8,128)(4,1)}, u32[]{:S(2)}) copy-start(pred[8,17]{0,1:T(8,128)(4,1)} %constant.149) | copy-start | bytes 412
  166.2 2.5 copy-start.3
  278.0 314.0 %collective-permute-start.5 = (f32[320,1,128]{2,0,1:T(8,128)S(1)}, f32[320,1,128]{2,0,1:T(8,128)S(1)}, u32[]{:S(2)}, u32[]{:S(2)}) collective-permute-start(f32[320,1,128]{2,0,1:T(8,128)S(1)} %pad.9), channel_id=1, source_target_pairs={{1,0},{2,1},{3,2},{4,3},{5,4},{6,5},{7,6},{8,7},{9,8},{10,9},{11,1... | collective-permute-start | bytes 491528 | tf_op jit(solution)/shard_map/ppermute | solution.py:12
Sparse Core Ops, SparseCore 0:
  132.4 457.7 all-reduce.3
where the time goes:
time: 602 us; the launch traced here: 600 us
  waiting for transfers between devices  319 us (53%)
  local copies, waits for them, and re-layouts  159 us (26%)
  other arithmetic  46 us (8%)
  starting transfers between devices  38.4 us (6%)
  matrix products  19.1 us (3%)
  between operations  14.3 us (2%)
    psum x1, waiting for transfers between devices, shards(): summed = lax.psum(kernel_local, ('rows', 'cols'))  310 us
    dynamic_update_slice x48, local copies, waits for them, and re-layouts, feature_one_level(): lax.dynamic_update_slice_in_dim(grad_ext, current + spread, offset, 2)  76.8 us
    dynamic_update_slice x48, local copies, waits for them, and re-layouts, correlate_one_level(): return lax.dynamic_update_slice_in_dim(volume, slab[:, None], level, 1)  29.6 us
    ppermute x2, starting transfers between devices, from_behind(): return lax.ppermute(shard, axis, pairs)  18.2 us
    ppermute x2, starting transfers between devices, padded_2(): before = lax.ppermute(last, axis, up)  17 us
    add x48, other arithmetic, feature_one_level(): grad_left + slab * shifted.reshape(groups, group_size, band_rows, tile_wi...  16.9 us
    unnamed x29, local copies, waits for them, and re-layouts  12.7 us
    conv_general_dilated x3, local copies, waits for them, and re-layouts, shards(): lax.conv_general_dilated(padded[None], flipped, (1, 1, 1), 'VALID', dimen...  12 us
  transfers between devices with their start and end apart: 7, of which 3 were waited for; matrix products, arithmetic and copies ran while one was open for 33% of the time, Pallas kernels for 0%

commit v1 on v0

v1 whole, which is shorter than its diff:
```python
import functools
import math

import jax
import jax.numpy as jnp
from jax import lax
from jax.experimental import pallas as pl
from jax.experimental.pallas import tpu as pltpu
from jax.sharding import PartitionSpec as P

MESH = pl.DeviceIdType.MESH
F32, BF16 = jnp.float32, jnp.bfloat16
ROWS, COLS = 32, 16
D, G, O, C, LANES = 48, 40, 32, 320, 128
TAPS = 9 * O
PLANE, DEEP = 32, 16
CHUNKS, CHUNK = 18, 16
HALF = C // 2


def plane_device(q, z):
    row = lax.rem(z, 8) * 4 + lax.rem(lax.div(q, 2), 4)
    return (row, lax.div(q, 8) * 4 + lax.div(z, 8) * 2 + lax.rem(q, 2))


def chunk_owner(j):
    return jnp.where(j < 16, 2 * j, jnp.where(j == 16, 1, 17))


def kernel(
    left, right, cot, weight, out_left, out_right, out_weight,
    wide, above, below, window, volume, grad_vol, left32, right32, border32, gl32, gr32, spill32,
    edge_send, edges, border_send, border, spill_send, spill, mixed, weight_t, terms, total,
    part1, part2, s_row, r_row, s_edge, r_edge, s_one, r_one, s1, r1, s2, r2, s3, r3,
):
    row, col = lax.axis_index("rows"), lax.axis_index("cols")
    core = lax.rem(col, 2)
    q = (lax.div(col, 4) * 4 + lax.rem(row, 4)) * 2 + core
    z = lax.rem(lax.div(col, 2), 2) * 8 + lax.div(row, 4)
    is_owner = jnp.logical_or(core == 0, jnp.logical_or(q == 1, q == 17))
    mine = jnp.where(core == 0, lax.div(q, 2), jnp.where(q == 1, 16, 17))
    lane = lax.broadcasted_iota(jnp.int32, (8, LANES), 1)
    lane32 = lax.broadcasted_iota(jnp.int32, (O, LANES), 1)

    def inside(dr, dc):
        ok = None
        for pos, step, count in ((row, dr, ROWS), (col, dc, COLS)):
            if step:
                here = pos > 0 if step < 0 else pos < count - 1
                ok = here if ok is None else jnp.logical_and(ok, here)
        return ok

    around = [(dr, dc) for dr in (-1, 0, 1) for dc in (-1, 0, 1) if (dr, dc) != (0, 0)]

    gate = pltpu.get_barrier_semaphore()
    expected = PLANE + DEEP - 2

    def greet(device):
        pl.semaphore_signal(gate, inc=1, device_id=device, device_id_type=MESH)

    for dr, dc in around:
        ok = inside(dr, dc)
        expected = expected + ok.astype(jnp.int32)
        pl.when(ok)(functools.partial(greet, (row + dr, col + dc)))

    @pl.loop(0, PLANE)
    def _(p):
        pl.when(p != q)(functools.partial(greet, plane_device(p, z)))

    @pl.loop(0, DEEP)
    def _(p):
        pl.when(p != z)(functools.partial(greet, plane_device(q, p)))

    def widen(src, dst, rows, step):
        @pl.loop(0, rows // step)
        def _(i):
            part = pl.ds(pl.multiple_of(i * step, step), step)
            dst[part] = src[part].astype(F32)

    widen(right, right32, C, 64)
    low, high = right32[pl.ds(0, HALF)], right32[pl.ds(HALF, HALF)]
    lane_half = lax.broadcasted_iota(jnp.int32, (HALF, LANES), 1)
    border_send[...] = jnp.where(lane_half >= 64, low, pltpu.roll(high, 64, 1)).astype(BF16)
    widen(cot, wide, O * D, 64)

    def edge_body(d, carry):
        first, last = carry
        t = wide[pl.ds(d, O, stride=D), :]
        first = jnp.where(lane32 == d, pltpu.roll(t, d, 1), first)
        last = jnp.where(lane32 == d, pltpu.roll(t, d + 1, 1), last)
        return first, last

    blank = jnp.zeros((O, LANES), F32)
    first, last = lax.fori_loop(0, D, edge_body, (blank, blank), unroll=4)
    edge_send[0] = last.astype(BF16)
    edge_send[1] = first.astype(BF16)

    pl.semaphore_wait(gate, expected)

    def remote(src, dst, send, recv, device):
        return pltpu.make_async_remote_copy(src, dst, send, recv, device_id=device, device_id_type=MESH)

    border_copy = remote(border_send, border, s_one.at[0], r_one.at[0], (row, col + 1))
    pl.when(inside(0, 1))(border_copy.start)
    edge_copies = []
    for side, dc in ((0, 1), (1, -1)):
        for dr in (-1, 0, 1):
            copy = remote(
                edge_send.at[side], edges.at[side, dr + 1],
                s_edge.at[side, dr + 1], r_edge.at[side, dr + 1], (row + dr, col + dc),
            )
            pl.when(inside(dr, dc))(copy.start)
            edge_copies.append((copy, inside(dr, dc), inside(-dr, -dc), edges.at[side, dr + 1]))
    down_copy = remote(cot, above, s_row.at[0], r_row.at[0], (row + 1, col))
    up_copy = remote(cot, below, s_row.at[1], r_row.at[1], (row - 1, col))
    pl.when(inside(1, 0))(down_copy.start)
    pl.when(inside(-1, 0))(up_copy.start)

    widen(left, left32, C, 64)
    for ref in (volume, grad_vol):
        ref[pl.ds(0, G)] = jnp.zeros((G, LANES), F32)
        ref[pl.ds((D + 1) * G, G + 8)] = jnp.zeros((G + 8, LANES), F32)

    @pl.loop(0, D)
    def _(d):
        grad_vol[pl.ds(pl.multiple_of((d + 1) * G, 8), G)] = jnp.zeros((G, LANES), F32)

    mixed[...] = jnp.zeros_like(mixed)
    weight_t[...] = jnp.zeros_like(weight_t)
    for a in range(3):
        mixed[pl.ds(0, TAPS), pl.ds(0, G)] = weight[a].astype(F32)
        weight_t[pl.ds(a * G, G)] = jnp.transpose(mixed[...])[:G]
    weights = weight_t[...][:, :TAPS].astype(BF16)
    terms[...] = jnp.zeros_like(terms)

    def settle(copy, ok, ref):
        pl.when(ok)(copy.wait_recv)

        @pl.when(jnp.logical_not(ok))
        def _():
            ref[...] = jnp.zeros_like(ref)

    settle(border_copy, inside(0, -1), border)
    arrived = border[...].astype(F32)
    border32[pl.ds(0, HALF)] = arrived
    border32[pl.ds(HALF, HALF)] = pltpu.roll(arrived, 64, 1)

    def group_rows(ref, block, k):
        return ref[pl.ds(block * 64 + k, 8, stride=8), :]

    @pl.loop(0, G // 8)
    def _(block):
        own = [group_rows(right32, block, k) for k in range(8)]
        far = [group_rows(border32, block, k) for k in range(8)]
        lefts = [group_rows(left32, block, k) for k in range(8)]

        def level(d, carry):
            inner = lane < LANES - d
            total_ = None
            for k in range(8):
                shifted = pltpu.roll(jnp.where(inner, own[k], far[k]), d, 1)
                product = lefts[k] * shifted
                total_ = product if total_ is None else total_ + product
            volume[pl.ds(pl.multiple_of((d + 1) * G + block * 8, 8), 8)] = total_ * 0.125
            return carry

        lax.fori_loop(0, D, level, 0, unroll=4)

    def windows(b):
        from_left, from_right = edges[0, b].astype(F32), edges[1, b].astype(F32)

        def body(d, carry):
            t = wide[pl.ds(d, O, stride=D), :]
            after = jnp.where(lane32 == 127, pltpu.roll(from_right, 127 - d, 1), pltpu.roll(t, 127, 1))
            before = jnp.where(lane32 == 0, pltpu.roll(from_left, lax.rem(LANES - d, LANES), 1), pltpu.roll(t, 1, 1))
            base = d * TAPS + b * 96
            window[pl.ds(pl.multiple_of(base, 32), O)] = after.astype(BF16)
            window[pl.ds(pl.multiple_of(base + 32, 32), O)] = t.astype(BF16)
            window[pl.ds(pl.multiple_of(base + 64, 32), O)] = before.astype(BF16)
            return carry

        lax.fori_loop(0, D, body, 0, unroll=2)

    for copy, _, ok, ref in edge_copies:
        settle(copy, ok, ref)
    windows(1)
    settle(down_copy, inside(-1, 0), above)
    widen(above, wide, O * D, 64)
    windows(2)
    settle(up_copy, inside(1, 0), below)
    widen(below, wide, O * D, 64)
    windows(0)

    def block_of(d):
        return window[pl.ds(pl.multiple_of(d * TAPS, 32), TAPS)]

    def term_body(t, carry):
        lhs = jnp.concatenate([block_of(t * 4 + s) for s in range(4)], axis=1)
        rhs = jnp.concatenate(
            [volume[pl.ds(pl.multiple_of((t * 4 + s) * G, 8), LANES)].astype(BF16) for s in range(4)], axis=1
        )
        terms[...] += lax.dot_general(lhs, rhs, (((1,), (1,)), ((), ())), preferred_element_type=F32)
        return carry

    lax.fori_loop(0, D // 4, term_body, 0)

    def scatter(j, slot, p):
        return remote(terms.at[pl.ds(pl.multiple_of(j * CHUNK, CHUNK), CHUNK)], part1.at[slot], s1.at[j], r1.at[slot], plane_device(p, z))

    def across(slot, p):
        return remote(part2.at[z], part2.at[slot], s2.at[p], r2.at[slot], plane_device(q, p))

    def spread(j, p):
        part = total.at[pl.ds(pl.multiple_of(j * CHUNK, CHUNK), CHUNK)]
        return remote(part, part, s3.at[p], r3.at[j], plane_device(p, z))

    def others(count, me, what):
        @pl.loop(0, count)
        def _(p):
            pl.when(p != me)(lambda: what(p))

    def chunks(what):
        @pl.loop(0, CHUNKS)
        def _(j):
            p = chunk_owner(j)
            pl.when(p != q)(lambda: what(j, p))

    chunks(lambda j, p: scatter(j, q, p).start())

    def volume_body(t, carry):
        rhs = jnp.concatenate([block_of(t * 2), block_of(t * 2 + 1)], axis=1)
        spread_ = jnp.dot(weights, rhs, preferred_element_type=F32)
        for s in range(2):
            part = pl.ds(pl.multiple_of((t * 2 + s) * G, 8), 3 * G)
            grad_vol[part] += spread_[: 3 * G, s * LANES : (s + 1) * LANES]
        return carry

    lax.fori_loop(0, D // 2, volume_body, 0, unroll=2)

    @pl.when(is_owner)
    def _():
        others(PLANE, q, lambda p: scatter(0, p, p).wait_recv())
        part1[q] = terms[pl.ds(pl.multiple_of(mine * CHUNK, CHUNK), CHUNK)]
        partial = part1[0]
        for p in range(1, PLANE):
            partial = partial + part1[p]
        part2[z] = partial
        others(DEEP, z, lambda p: across(z, p).start())

    @pl.loop(0, G // 8)
    def _(block):
        own = [group_rows(right32, block, k) for k in range(8)]
        far = [group_rows(border32, block, k) for k in range(8)]
        lefts = [group_rows(left32, block, k) for k in range(8)]

        def level(d, carry):
            gl, gr, sp = carry
            inner = lane < LANES - d
            slab = grad_vol[pl.ds(pl.multiple_of((d + 1) * G + block * 8, 8), 8)]
            back = lax.rem(LANES - d, LANES)
            moved = pltpu.roll(slab, back, 1)
            here, there = jnp.where(inner, moved, 0.0), jnp.where(inner, 0.0, moved)
            gl = [gl[k] + slab * pltpu.roll(jnp.where(inner, own[k], far[k]), d, 1) for k in range(8)]
            turned = [pltpu.roll(lefts[k], back, 1) for k in range(8)]
            gr = [gr[k] + here * turned[k] for k in range(8)]
            sp = [sp[k] + there * turned[k] for k in range(8)]
            return gl, gr, sp

        zeros = [jnp.zeros((8, LANES), F32)] * 8
        gl, gr, sp = lax.fori_loop(0, D, level, (zeros, zeros, zeros), unroll=2)
        for k in range(8):
            part = pl.ds(block * 64 + k, 8, stride=8)
            gl32[part, :] = gl[k] * 0.125
            gr32[part, :] = gr[k] * 0.125
            spill32[part, :] = sp[k] * 0.125

    spill_send[...] = jnp.where(lane_half >= 64, spill32[pl.ds(0, HALF)], pltpu.roll(spill32[pl.ds(HALF, HALF)], 64, 1))
    spill_copy = remote(spill_send, spill, s_one.at[1], r_one.at[1], (row, col - 1))
    pl.when(inside(0, -1))(spill_copy.start)

    @pl.when(is_owner)
    def _():
        others(DEEP, z, lambda p: across(p, p).wait_recv())
        whole = part2[0]
        for p in range(1, DEEP):
            whole = whole + part2[p]
        total[pl.ds(pl.multiple_of(mine * CHUNK, CHUNK), CHUNK)] = whole
        others(PLANE, q, lambda p: spread(mine, p).start())

    out_left[...] = gl32[...].astype(BF16)
    settle(spill_copy, inside(0, 1), spill)
    extra = spill[...]
    upper = lane_half >= LANES - (D - 1)
    out_right[pl.ds(0, HALF)] = (gr32[pl.ds(0, HALF)] + jnp.where(upper, extra, 0.0)).astype(BF16)
    out_right[pl.ds(HALF, HALF)] = (
        gr32[pl.ds(HALF, HALF)] + jnp.where(upper, pltpu.roll(extra, 64, 1), 0.0)
    ).astype(BF16)

    chunks(lambda j, p: spread(j, p).wait_recv())
    scale = 1.0 / math.sqrt(D * ROWS * COLS * LANES)
    summed = total[...] * scale
    for a in range(3):
        turned = summed if a == 0 else pltpu.roll(summed, LANES - a * G, 1)
        out_weight[pl.ds(a * TAPS, TAPS)] = turned[:, :G]

    pl.when(inside(0, 1))(border_copy.wait_send)
    for copy, ok, _, _ in edge_copies:
        pl.when(ok)(copy.wait_send)
    pl.when(inside(1, 0))(down_copy.wait_send)
    pl.when(inside(-1, 0))(up_copy.wait_send)
    pl.when(inside(0, -1))(spill_copy.wait_send)
    chunks(lambda j, p: scatter(j, q, p).wait_send())

    @pl.when(is_owner)
    def _():
        others(DEEP, z, lambda p: across(z, p).wait_send())
        others(PLANE, q, lambda p: spread(mine, p).wait_send())


def shards(left_feat, right_feat, grad_out, conv_weight):
    vmem = pl.BlockSpec(memory_space=pltpu.VMEM)
    dma = pltpu.SemaphoreType.DMA
    weight = jnp.transpose(conv_weight, (2, 3, 4, 0, 1)).reshape(3, TAPS, G)
    padded = (D + 2) * G + 8
    wide_rows = lambda rows: pltpu.VMEM((rows, LANES), F32)
    half_rows = lambda rows: pltpu.VMEM((rows, LANES), BF16)
    grad_left, grad_right, grad_weight = pl.pallas_call(
        kernel,
        out_shape=(
            jax.ShapeDtypeStruct((C, LANES), BF16),
            jax.ShapeDtypeStruct((C, LANES), BF16),
            jax.ShapeDtypeStruct((3 * TAPS, G), F32),
        ),
        in_specs=[vmem] * 4,
        out_specs=(vmem,) * 3,
        scratch_shapes=[
            wide_rows(O * D), half_rows(O * D), half_rows(O * D), half_rows(D * TAPS),
            wide_rows(padded), wide_rows(padded),
            wide_rows(C), wide_rows(C), wide_rows(C), wide_rows(C), wide_rows(C), wide_rows(C),
            pltpu.VMEM((2, O, LANES), BF16), pltpu.VMEM((2, 3, O, LANES), BF16),
            half_rows(HALF), half_rows(HALF), wide_rows(HALF), wide_rows(HALF),
            wide_rows(384), pltpu.VMEM((LANES, 384), F32), wide_rows(TAPS), wide_rows(TAPS),
            pltpu.VMEM((PLANE, CHUNK, LANES), F32), pltpu.VMEM((DEEP, CHUNK, LANES), F32),
            dma((2,)), dma((2,)), dma((2, 3)), dma((2, 3)), dma((2,)), dma((2,)),
            dma((CHUNKS,)), dma((PLANE,)), dma((DEEP,)), dma((DEEP,)), dma((PLANE,)), dma((CHUNKS,)),
        ],
        compiler_params=pltpu.CompilerParams(
            collective_id=0, has_side_effects=True, vmem_limit_bytes=40 * 1024 * 1024
        ),
        cost_estimate=pl.CostEstimate(flops=10**9, bytes_accessed=4 * 10**6, transcendentals=0),
    )(
        left_feat.reshape(C, LANES),
        right_feat.reshape(C, LANES),
        grad_out.reshape(O * D, LANES),
        weight,
    )
    return (
        grad_left.reshape(C, 1, LANES),
        grad_right.reshape(C, 1, LANES),
        jnp.transpose(grad_weight.reshape(3, 3, 3, O, G), (3, 4, 0, 1, 2)),
    )


def solution(mesh):
    placed = (P(None, "rows", "cols"), P(None, "rows", "cols"), P(None, None, "rows", "cols"), P())
    return jax.shard_map(
        shards,
        mesh=mesh,
        in_specs=placed,
        out_specs=(P(None, "rows", "cols"), P(None, "rows", "cols"), P()),
        check_vma=False,
    )
```

time: 602 us -> 80.3 us (0.13)
  waiting for transfers between devices: 319 us -> 0 us
  local copies, waits for them, and re-layouts: 159 us -> 5.73 us
  Pallas kernels: 0 us -> 73.6 us
  other arithmetic: 46 us -> 0 us
  starting transfers between devices: 38.4 us -> 0 us
  matrix products: 19.1 us -> 0 us
  between operations: 14.3 us -> 0.65 us
    psum x1 -> x0, waiting for transfers between devices: 310 us -> none  [shards(): summed = lax.psum(kernel_local, ('rows', 'cols'))]
    dynamic_update_slice x96 -> x0, local copies, waits for them, and re-layouts: 106 us -> none  [the longest x48 76.8 us: feature_one_level(): lax.dynamic_update_slice_in_dim(grad_ext, current + spread, offset, 2)]
    pallas_call x0 -> x1, Pallas kernels: none -> 73.6 us  [shards(): pl.pallas_call(kernel, out_shape=(jax.ShapeDtypeStruct((C, LANES), BF16),...]
    ppermute x6 -> x0, starting transfers between devices: 38.4 us -> none  [the longest x2 18.2 us: from_behind(): return lax.ppermute(shard, axis, pairs)]
    add x96 -> x0, other arithmetic: 18.4 us -> none  [the longest x48 16.9 us: feature_one_level(): grad_left + slab * shifted.reshape(groups, group_size, band_rows, tile_wi...]
    conv_general_dilated x3 -> x0, local copies, waits for them, and re-layouts: 12 us -> none  [shards(): lax.conv_general_dilated(padded[None], flipped, (1, 1, 1), 'VALID', dimen...]
    mul x98 -> x0, other arithmetic: 10.4 us -> none  [the longest x48 8.31 us: correlate_one_level(): left_wide * shifted]
    conv_general_dilated x1 -> x0, matrix products: 10 us -> none  [shards(): lax.conv_general_dilated(padded[None], flipped, (1, 1, 1), 'VALID', dimen...]
  transfers between devices with their start and end apart: 7 -> 0, of which waited for: 3 -> 0; matrix products, arithmetic and copies ran while one was open for 33% -> 0% of each run, Pallas kernels for 0% -> 0%
where the time goes in v1:
time: 80.3 us; the launch traced here: 80 us
  Pallas kernels  73.6 us (92%)
  local copies, waits for them, and re-layouts  5.73 us (7%)
    pallas_call x1, Pallas kernels, shards(): pl.pallas_call(kernel, out_shape=(jax.ShapeDtypeStruct((C, LANES), BF16),...  73.6 us
    unnamed x11, local copies, waits for them, and re-layouts  5.73 us

profile of v1, /device:TPU:1, one launch (start us, length us, event | category | flops | bytes accessed | tf_op | source)
XLA Modules:
  0.0 80.0 jit_solution(3646956243469461214)
XLA Ops:
  0.6 0.0 copy-start
  0.6 1.0 %copy-done = bf16[32,48,1,128]{3,1,2,0:T(8,128)(2,1)S(1)} copy-done((bf16[32,48,1,128]{3,1,2,0:T(8,128)(2,1)S(1)}, bf16[32,48,1,128]{3,1,2,0:T(8,128)(2,1)}, u32[]{:S(2)}) %copy-start) | copy-done | bytes 393240
  1.6 0.0 copy-start.1
  1.6 0.9 %copy-done.1 = bf16[32,40,3,3,3]{1,0,4,3,2:T(8,128)(2,1)S(1)} copy-done((bf16[32,40,3,3,3]{1,0,4,3,2:T(8,128)(2,1)S(1)}, bf16[32,40,3,3,3]{1,0,4,3,2:T(8,128)(2,1)}, u32[]{:S(2)}) %copy-start.1) | copy-done | bytes 69144
  2.6 0.0 copy-start.2
  2.6 0.9 %copy-done.2 = bf16[320,1,128]{2,0,1:T(8,128)(2,1)S(1)} copy-done((bf16[320,1,128]{2,0,1:T(8,128)(2,1)S(1)}, bf16[320,1,128]{2,0,1:T(8,128)(2,1)}, u32[]{:S(2)}) %copy-start.2) | copy-done | bytes 81944
  3.5 0.0 copy-start.3
  3.5 0.9 %copy-done.3 = bf16[320,1,128]{2,0,1:T(8,128)(2,1)S(1)} copy-done((bf16[320,1,128]{2,0,1:T(8,128)(2,1)S(1)}, bf16[320,1,128]{2,0,1:T(8,128)(2,1)}, u32[]{:S(2)}) %copy-start.3) | copy-done | bytes 81944
  4.3 73.6 %shard_map.67 = (bf16[320,128]{1,0:T(8,128)(2,1)S(1)}, bf16[320,128]{1,0:T(8,128)(2,1)S(1)}, f32[864,40]{1,0:T(8,128)S(1)}) custom-call(bf16[320,128]{1,0:T(8,128)(2,1)S(1)} %bitcast.16, bf16[320,128]{1,0:T(8,128)(2,1)S(1)} %bitcast.17, bf16[1536,128]{1,0:T(8,128)(2,1)S(1)} %bitcast.14, bf16[3,288,40]{2,1,0:T(8,128)(2,1)S(1)} %bitcast.15), custom_call_target="tpu_custom_call" | custom-call | flops 1000000000 | bytes 4000000 | tf_op jit(solution)/shard_map/pallas_call | solution.py:327
  78.0 0.6 copy.10
  78.6 0.6 copy.11
  79.2 0.8 copy.12
Async XLA Ops:
  0.6 1.0 %copy-start = (bf16[32,48,1,128]{3,1,2,0:T(8,128)(2,1)S(1)}, bf16[32,48,1,128]{3,1,2,0:T(8,128)(2,1)}, u32[]{:S(2)}) copy-start(bf16[32,48,1,128]{3,1,2,0:T(8,128)(2,1)} %param.6) | copy-start | bytes 1179652
  1.6 0.9 %copy-start.1 = (bf16[32,40,3,3,3]{1,0,4,3,2:T(8,128)(2,1)S(1)}, bf16[32,40,3,3,3]{1,0,4,3,2:T(8,128)(2,1)}, u32[]{:S(2)}) copy-start(bf16[32,40,3,3,3]{1,0,4,3,2:T(8,128)(2,1)} %param.7) | copy-start | bytes 207364
  2.6 0.9 %copy-start.2 = (bf16[320,1,128]{2,0,1:T(8,128)(2,1)S(1)}, bf16[320,1,128]{2,0,1:T(8,128)(2,1)}, u32[]{:S(2)}) copy-start(bf16[320,1,128]{2,0,1:T(8,128)(2,1)} %param.4) | copy-start | bytes 245764
  3.5 0.9 %copy-start.3 = (bf16[320,1,128]{2,0,1:T(8,128)(2,1)S(1)}, bf16[320,1,128]{2,0,1:T(8,128)(2,1)}, u32[]{:S(2)}) copy-start(bf16[320,1,128]{2,0,1:T(8,128)(2,1)} %param.5) | copy-start | bytes 245764

commit v2 on v1

--- a/solution.py
+++ b/solution.py
@@ -28,10 +28,11 @@
 
 
 def kernel(
-    left, right, cot, weight, out_left, out_right, out_weight,
-    wide, above, below, window, volume, grad_vol, left32, right32, border32, gl32, gr32, spill32,
-    edge_send, edges, border_send, border, spill_send, spill, mixed, weight_t, terms, total,
-    part1, part2, s_row, r_row, s_edge, r_edge, s_one, r_one, s1, r1, s2, r2, s3, r3,
+    left_in, right_in, cot_in, weight_in, out_left, out_right, out_weight,
+    left, right, cot, weight, wide, above, below, window, volume, grad_vol, left32, right32, gl32, gr32, spill32,
+    by_tap, by_tap_bf, ext, moved_right, moved_left, near, edge32, edge_send, edges, border_send, border,
+    spill_send, spill, mixed, weight_t, terms, total,
+    part1, part2, s_in, s_row, r_row, s_edge, r_edge, s_one, r_one, s1, r1, s2, r2, s3, r3,
 ):
     row, col = lax.axis_index("rows"), lax.axis_index("cols")
     core = lax.rem(col, 2)
@@ -71,16 +72,25 @@
     def _(p):
         pl.when(p != z)(functools.partial(greet, plane_device(q, p)))
 
+    loads = [
+        pltpu.make_async_copy(src, dst, s_in.at[i])
+        for i, (src, dst) in enumerate(((right_in, right), (cot_in, cot), (left_in, left), (weight_in, weight)))
+    ]
+    for load in loads:
+        load.start()
+
     def widen(src, dst, rows, step):
         @pl.loop(0, rows // step)
         def _(i):
             part = pl.ds(pl.multiple_of(i * step, step), step)
             dst[part] = src[part].astype(F32)
 
+    loads[0].wait()
     widen(right, right32, C, 64)
     low, high = right32[pl.ds(0, HALF)], right32[pl.ds(HALF, HALF)]
     lane_half = lax.broadcasted_iota(jnp.int32, (HALF, LANES), 1)
     border_send[...] = jnp.where(lane_half >= 64, low, pltpu.roll(high, 64, 1)).astype(BF16)
+    loads[1].wait()
     widen(cot, wide, O * D, 64)
 
     def edge_body(d, carry):
@@ -111,11 +121,13 @@
             )
             pl.when(inside(dr, dc))(copy.start)
             edge_copies.append((copy, inside(dr, dc), inside(-dr, -dc), edges.at[side, dr + 1]))
-    down_copy = remote(cot, above, s_row.at[0], r_row.at[0], (row + 1, col))
-    up_copy = remote(cot, below, s_row.at[1], r_row.at[1], (row - 1, col))
+    down_copy = remote(cot_in, above, s_row.at[0], r_row.at[0], (row + 1, col))
+    up_copy = remote(cot_in, below, s_row.at[1], r_row.at[1], (row - 1, col))
     pl.when(inside(1, 0))(down_copy.start)
     pl.when(inside(-1, 0))(up_copy.start)
 
+    loads[2].wait()
+    loads[3].wait()
     widen(left, left32, C, 64)
     for ref in (volume, grad_vol):
         ref[pl.ds(0, G)] = jnp.zeros((G, LANES), F32)
@@ -128,7 +140,9 @@
     mixed[...] = jnp.zeros_like(mixed)
     weight_t[...] = jnp.zeros_like(weight_t)
     for a in range(3):
-        mixed[pl.ds(0, TAPS), pl.ds(0, G)] = weight[a].astype(F32)
+        for b in range(3):
+            for c in range(3):
+                mixed[pl.ds(c * 96 + b * O, O), pl.ds(0, G)] = weight[a, pl.ds((b * 3 + c) * O, O), :].astype(F32)
         weight_t[pl.ds(a * G, G)] = jnp.transpose(mixed[...])[:G]
     weights = weight_t[...][:, :TAPS].astype(BF16)
     terms[...] = jnp.zeros_like(terms)
@@ -140,56 +154,105 @@
         def _():
             ref[...] = jnp.zeros_like(ref)
 
+    def regroup(ref):
+        return jnp.concatenate([ref[pl.ds(k, G, stride=8), :] for k in range(8)], axis=0)
+
+    by_tap[...] = regroup(left32)
+    by_tap_bf[...] = by_tap[...].astype(BF16)
+    ext[:, pl.ds(LANES, LANES)] = regroup(right32).astype(BF16)
+    source = lax.broadcasted_iota(jnp.int32, (2 * LANES, LANES), 0) - lax.broadcasted_iota(jnp.int32, (2 * LANES, LANES), 1)
+    ring = source[:LANES]
+
+    def pick(hit):
+        return jnp.where(hit, 1.0, 0.0).astype(BF16)
+
+    def turn_body(t, carry):
+        d = t * 2
+        rule = jnp.concatenate([pick(jnp.logical_or(ring == d + s, ring == d + s - LANES)) for s in range(2)], axis=1)
+        turned = jnp.dot(by_tap_bf[...], rule, preferred_element_type=F32)
+        for s in range(2):
+            moved_left[pl.ds(pl.multiple_of((d + s) * C, 8), C)] = turned[:, s * LANES : (s + 1) * LANES]
+        return carry
+
+    lax.fori_loop(0, D // 2, turn_body, 0, unroll=8)
+
+    def centre(b):
+        def body(d, carry):
+            base = pl.multiple_of(d * TAPS + 96 + b * O, 32)
+            window[pl.ds(base, O)] = wide[pl.ds(d, O, stride=D), :].astype(BF16)
+            return carry
+
+        lax.fori_loop(0, D, body, 0, unroll=4)
+
+    centre(1)
+    for copy, _, ok, ref in edge_copies:
+        settle(copy, ok, ref)
+    for b in range(3):
+        from_left, from_right = edges[0, b].astype(F32), edges[1, b].astype(F32)
+        edge32[pl.ds(b * O, O)] = jnp.where(lane32 < 64, from_left, pltpu.roll(from_right, 64, 1))
+    row_j = lax.broadcasted_iota(jnp.int32, (LANES, LANES), 0)
+    col_w = lax.broadcasted_iota(jnp.int32, (LANES, LANES), 1)
+    near[pl.ds(0, LANES), pl.ds(0, LANES)] = pick(row_j == col_w + 1)
+    near[pl.ds(0, LANES), pl.ds(LANES, LANES)] = pick(row_j == col_w - 1)
+    near[pl.ds(LANES, LANES), pl.ds(0, LANES)] = pick(jnp.logical_and(row_j >= 64, col_w == LANES - 1))
+    near[pl.ds(LANES, LANES), pl.ds(LANES, LANES)] = pick(jnp.logical_and(row_j < 64, col_w == 0))
+    lane96 = lax.broadcasted_iota(jnp.int32, (96, LANES), 1)
+
+    def windows_body(t, carry):
+        rows = []
+        for s in range(4):
+            d = t * 4 + s
+            hit = jnp.logical_or(lane96 == d, lane96 == d + 64)
+            rim = jnp.where(hit, edge32[...], 0.0).astype(BF16)
+            rows.append(jnp.concatenate([window[pl.ds(pl.multiple_of(d * TAPS + 96, 32), 96)], rim], axis=1))
+        sides = jnp.dot(jnp.concatenate(rows, axis=0), near[...], preferred_element_type=F32).astype(BF16)
+        for s in range(4):
+            d = t * 4 + s
+            window[pl.ds(pl.multiple_of(d * TAPS, 32), 96)] = sides[s * 96 : (s + 1) * 96, :LANES]
+            window[pl.ds(pl.multiple_of(d * TAPS + 192, 32), 96)] = sides[s * 96 : (s + 1) * 96, LANES:]
+        return carry
+
+    def rows_part():
+        pl.when(inside(-1, 0))(down_copy.wait_recv)
+        widen(above, wide, O * D, 64)
+        centre(2)
+        pl.when(inside(1, 0))(up_copy.wait_recv)
+        widen(below, wide, O * D, 64)
+        centre(0)
+        lax.fori_loop(0, D // 4, windows_body, 0)
+
+    @pl.when(row == 0)
+    def _():
+        above[...] = jnp.zeros_like(above)
+
+    @pl.when(row == ROWS - 1)
+    def _():
+        below[...] = jnp.zeros_like(below)
+
+    late = z >= 4
+    pl.when(late)(rows_part)
+
     settle(border_copy, inside(0, -1), border)
     arrived = border[...].astype(F32)
-    border32[pl.ds(0, HALF)] = arrived
-    border32[pl.ds(HALF, HALF)] = pltpu.roll(arrived, 64, 1)
-
-    def group_rows(ref, block, k):
-        return ref[pl.ds(block * 64 + k, 8, stride=8), :]
-
-    @pl.loop(0, G // 8)
-    def _(block):
-        own = [group_rows(right32, block, k) for k in range(8)]
-        far = [group_rows(border32, block, k) for k in range(8)]
-        lefts = [group_rows(left32, block, k) for k in range(8)]
-
-        def level(d, carry):
-            inner = lane < LANES - d
-            total_ = None
-            for k in range(8):
-                shifted = pltpu.roll(jnp.where(inner, own[k], far[k]), d, 1)
-                product = lefts[k] * shifted
-                total_ = product if total_ is None else total_ + product
-            volume[pl.ds(pl.multiple_of((d + 1) * G + block * 8, 8), 8)] = total_ * 0.125
-            return carry
-
-        lax.fori_loop(0, D, level, 0, unroll=4)
-
-    def windows(b):
-        from_left, from_right = edges[0, b].astype(F32), edges[1, b].astype(F32)
-
-        def body(d, carry):
-            t = wide[pl.ds(d, O, stride=D), :]
-            after = jnp.where(lane32 == 127, pltpu.roll(from_right, 127 - d, 1), pltpu.roll(t, 127, 1))
-            before = jnp.where(lane32 == 0, pltpu.roll(from_left, lax.rem(LANES - d, LANES), 1), pltpu.roll(t, 1, 1))
-            base = d * TAPS + b * 96
-            window[pl.ds(pl.multiple_of(base, 32), O)] = after.astype(BF16)
-            window[pl.ds(pl.multiple_of(base + 32, 32), O)] = t.astype(BF16)
-            window[pl.ds(pl.multiple_of(base + 64, 32), O)] = before.astype(BF16)
-            return carry
-
-        lax.fori_loop(0, D, body, 0, unroll=2)
-
-    for copy, _, ok, ref in edge_copies:
-        settle(copy, ok, ref)
-    windows(1)
-    settle(down_copy, inside(-1, 0), above)
-    widen(above, wide, O * D, 64)
-    windows(2)
-    settle(up_copy, inside(1, 0), below)
-    widen(below, wide, O * D, 64)
-    windows(0)
+    right32[pl.ds(0, HALF)] = arrived
+    right32[pl.ds(HALF, HALF)] = pltpu.roll(arrived, 64, 1)
+    ext[:, pl.ds(0, LANES)] = regroup(right32).astype(BF16)
+
+    def volume_pair(t, carry):
+        d = t * 2
+        rule = jnp.concatenate([pick(source == LANES - d - s) for s in range(2)], axis=1)
+        moved = jnp.dot(ext[...], rule, preferred_element_type=F32)
+        for s in range(2):
+            part = moved[:, s * LANES : (s + 1) * LANES]
+            moved_right[pl.ds(pl.multiple_of((d + s) * C, 8), C)] = part
+            slab = by_tap[pl.ds(0, G)] * part[:G]
+            for k in range(1, 8):
+                slab = slab + by_tap[pl.ds(k * G, G)] * part[k * G : (k + 1) * G]
+            volume[pl.ds(pl.multiple_of((d + s + 1) * G, 8), G)] = slab * 0.125
+        return carry
+
+    lax.fori_loop(0, D // 2, volume_pair, 0, unroll=8)
+    pl.when(jnp.logical_not(late))(rows_part)
 
     def block_of(d):
         return window[pl.ds(pl.multiple_of(d * TAPS, 32), TAPS)]
@@ -202,7 +265,7 @@
         terms[...] += lax.dot_general(lhs, rhs, (((1,), (1,)), ((), ())), preferred_element_type=F32)
         return carry
 
-    lax.fori_loop(0, D // 4, term_body, 0)
+    lax.fori_loop(0, D // 4, term_body, 0, unroll=6)
 
     def scatter(j, slot, p):
         return remote(terms.at[pl.ds(pl.multiple_of(j * CHUNK, CHUNK), CHUNK)], part1.at[slot], s1.at[j], r1.at[slot], plane_device(p, z))
@@ -235,7 +298,7 @@
             grad_vol[part] += spread_[: 3 * G, s * LANES : (s + 1) * LANES]
         return carry
 
-    lax.fori_loop(0, D // 2, volume_body, 0, unroll=2)
+    lax.fori_loop(0, D // 2, volume_body, 0, unroll=8)
 
     @pl.when(is_owner)
     def _():
@@ -249,25 +312,21 @@
 
     @pl.loop(0, G // 8)
     def _(block):
-        own = [group_rows(right32, block, k) for k in range(8)]
-        far = [group_rows(border32, block, k) for k in range(8)]
-        lefts = [group_rows(left32, block, k) for k in range(8)]
-
         def level(d, carry):
             gl, gr, sp = carry
             inner = lane < LANES - d
             slab = grad_vol[pl.ds(pl.multiple_of((d + 1) * G + block * 8, 8), 8)]
-            back = lax.rem(LANES - d, LANES)
-            moved = pltpu.roll(slab, back, 1)
+            moved = pltpu.roll(slab, lax.rem(LANES - d, LANES), 1)
             here, there = jnp.where(inner, moved, 0.0), jnp.where(inner, 0.0, moved)
-            gl = [gl[k] + slab * pltpu.roll(jnp.where(inner, own[k], far[k]), d, 1) for k in range(8)]
-            turned = [pltpu.roll(lefts[k], back, 1) for k in range(8)]
+            at = [pl.ds(pl.multiple_of(d * C + k * G + block * 8, 8), 8) for k in range(8)]
+            gl = [gl[k] + slab * moved_right[at[k]] for k in range(8)]
+            turned = [moved_left[at[k]] for k in range(8)]
             gr = [gr[k] + here * turned[k] for k in range(8)]
             sp = [sp[k] + there * turned[k] for k in range(8)]
             return gl, gr, sp
 
         zeros = [jnp.zeros((8, LANES), F32)] * 8
-        gl, gr, sp = lax.fori_loop(0, D, level, (zeros, zeros, zeros), unroll=2)
+        gl, gr, sp = lax.fori_loop(0, D, level, (zeros, zeros, zeros), unroll=16)
         for k in range(8):
             part = pl.ds(block * 64 + k, 8, stride=8)
             gl32[part, :] = gl[k] * 0.125
@@ -301,7 +360,9 @@
     summed = total[...] * scale
     for a in range(3):
         turned = summed if a == 0 else pltpu.roll(summed, LANES - a * G, 1)
-        out_weight[pl.ds(a * TAPS, TAPS)] = turned[:, :G]
+        for b in range(3):
+            for c in range(3):
+                out_weight[pl.ds(a * TAPS + (b * 3 + c) * O, O)] = turned[c * 96 + b * O : c * 96 + (b + 1) * O, :G]
 
     pl.when(inside(0, 1))(border_copy.wait_send)
     for copy, ok, _, _ in edge_copies:
@@ -331,21 +392,24 @@
             jax.ShapeDtypeStruct((C, LANES), BF16),
             jax.ShapeDtypeStruct((3 * TAPS, G), F32),
         ),
-        in_specs=[vmem] * 4,
+        in_specs=[pl.BlockSpec(memory_space=pl.ANY)] * 4,
         out_specs=(vmem,) * 3,
         scratch_shapes=[
+            half_rows(C), half_rows(C), half_rows(O * D), pltpu.VMEM((3, TAPS, G), BF16),
             wide_rows(O * D), half_rows(O * D), half_rows(O * D), half_rows(D * TAPS),
             wide_rows(padded), wide_rows(padded),
-            wide_rows(C), wide_rows(C), wide_rows(C), wide_rows(C), wide_rows(C), wide_rows(C),
+            wide_rows(C), wide_rows(C), wide_rows(C), wide_rows(C), wide_rows(C),
+            wide_rows(C), half_rows(C), pltpu.VMEM((C, 2 * LANES), BF16), wide_rows(D * C), wide_rows(D * C),
+            pltpu.VMEM((2 * LANES, 2 * LANES), BF16), wide_rows(96),
             pltpu.VMEM((2, O, LANES), BF16), pltpu.VMEM((2, 3, O, LANES), BF16),
             half_rows(HALF), half_rows(HALF), wide_rows(HALF), wide_rows(HALF),
             wide_rows(384), pltpu.VMEM((LANES, 384), F32), wide_rows(TAPS), wide_rows(TAPS),
             pltpu.VMEM((PLANE, CHUNK, LANES), F32), pltpu.VMEM((DEEP, CHUNK, LANES), F32),
-            dma((2,)), dma((2,)), dma((2, 3)), dma((2, 3)), dma((2,)), dma((2,)),
+            dma((4,)), dma((2,)), dma((2,)), dma((2, 3)), dma((2, 3)), dma((2,)), dma((2,)),
             dma((CHUNKS,)), dma((PLANE,)), dma((DEEP,)), dma((DEEP,)), dma((PLANE,)), dma((CHUNKS,)),
         ],
         compiler_params=pltpu.CompilerParams(
-            collective_id=0, has_side_effects=True, vmem_limit_bytes=40 * 1024 * 1024
+            collective_id=0, has_side_effects=True, vmem_limit_bytes=56 * 1024 * 1024
         ),
         cost_estimate=pl.CostEstimate(flops=10**9, bytes_accessed=4 * 10**6, transcendentals=0),
     )(

time: 80.3 us -> 62.6 us (0.78)
  Pallas kernels: 73.6 us -> 57.7 us
  local copies, waits for them, and re-layouts: 5.73 us -> 4 us
    pallas_call x1, Pallas kernels: 73.6 us -> 57.7 us  [shards(): pl.pallas_call(kernel, out_shape=(jax.ShapeDtypeStruct((C, LANES), BF16),...]
    unnamed x11 -> x5, local copies, waits for them, and re-layouts: 5.73 us -> 4 us
where the time goes in v2:
time: 62.6 us; the launch traced here: 62.3 us
  Pallas kernels  57.7 us (92%)
  local copies, waits for them, and re-layouts  4 us (6%)
  between operations  0.65 us (1%)
    pallas_call x1, Pallas kernels, shards(): pl.pallas_call(kernel, out_shape=(jax.ShapeDtypeStruct((C, LANES), BF16),...  57.7 us
    unnamed x5, local copies, waits for them, and re-layouts  4 us

profile of v2, /device:TPU:1, one launch (start us, length us, event | category | flops | bytes accessed | tf_op | source)
XLA Modules:
  0.0 62.3 jit_solution(16646876857560083803)
XLA Ops:
  0.6 57.7 %shard_map.67 = (bf16[320,128]{1,0:T(8,128)(2,1)}, bf16[320,128]{1,0:T(8,128)(2,1)}, f32[864,40]{1,0:T(8,128)}) custom-call(bf16[320,128]{1,0:T(8,128)(2,1)} %bitcast.16, bf16[320,128]{1,0:T(8,128)(2,1)} %bitcast.17, bf16[1536,128]{1,0:T(8,128)(2,1)} %bitcast.14, bf16[3,288,40]{2,1,0:T(8,128)(2,1)} %bitcast.15), custom_call_target="tpu_custom_call" | custom-call | flops 1000000000 | bytes 4000000 | tf_op jit(solution)/shard_map/pallas_call | solution.py:388
  58.3 0.0 copy-start
  58.3 1.6 %copy.10 = bf16[320,1,128]{2,0,1:T(8,128)(2,1)} copy(bf16[320,1,128]{2,0,1:T(8,128)(2,1)} %bitcast.13) | data formatting | bytes 163840
  59.9 0.0 copy-done
  59.9 0.6 %copy.11 = bf16[320,1,128]{2,0,1:T(8,128)(2,1)} copy(bf16[320,1,128]{2,0,1:T(8,128)(2,1)S(1)} %bitcast.12) | data formatting | bytes 163840
  60.5 1.8 %copy.12 = f32[32,40,3,3,3]{1,0,4,3,2:T(8,128)} copy(f32[32,40,3,3,3]{1,0,4,3,2:T(8,128)} %bitcast.11) | data formatting | bytes 276480
Async XLA Ops:
  58.3 1.6 %copy-start = (bf16[320,128]{1,0:T(8,128)(2,1)S(1)}, bf16[320,128]{1,0:T(8,128)(2,1)}, u32[]{:S(2)}) copy-start(bf16[320,128]{1,0:T(8,128)(2,1)} %get-tuple-element.7) | copy-start | bytes 245764

commit v3 on v2

--- a/solution.py
+++ b/solution.py
@@ -19,12 +19,10 @@
 
 
 def plane_device(q, z):
+    if isinstance(q, int):
+        return (lax.rem(z, 8) * 4 + q // 2 % 4, q // 8 * 4 + lax.div(z, 8) * 2 + q % 2)
     row = lax.rem(z, 8) * 4 + lax.rem(lax.div(q, 2), 4)
     return (row, lax.div(q, 8) * 4 + lax.div(z, 8) * 2 + lax.rem(q, 2))
-
-
-def chunk_owner(j):
-    return jnp.where(j < 16, 2 * j, jnp.where(j == 16, 1, 17))
 
 
 def kernel(
@@ -268,25 +266,23 @@
     lax.fori_loop(0, D // 4, term_body, 0, unroll=6)
 
     def scatter(j, slot, p):
-        return remote(terms.at[pl.ds(pl.multiple_of(j * CHUNK, CHUNK), CHUNK)], part1.at[slot], s1.at[j], r1.at[slot], plane_device(p, z))
+        return remote(terms.at[pl.ds(j * CHUNK, CHUNK)], part1.at[slot], s1.at[j], r1.at[slot], plane_device(p, z))
 
     def across(slot, p):
         return remote(part2.at[z], part2.at[slot], s2.at[p], r2.at[slot], plane_device(q, p))
 
     def spread(j, p):
-        part = total.at[pl.ds(pl.multiple_of(j * CHUNK, CHUNK), CHUNK)]
+        part = total.at[pl.ds(j * CHUNK, CHUNK)]
         return remote(part, part, s3.at[p], r3.at[j], plane_device(p, z))
 
     def others(count, me, what):
-        @pl.loop(0, count)
-        def _(p):
-            pl.when(p != me)(lambda: what(p))
+        for p in range(count):
+            pl.when(p != me)(functools.partial(what, p))
 
     def chunks(what):
-        @pl.loop(0, CHUNKS)
-        def _(j):
-            p = chunk_owner(j)
-            pl.when(p != q)(lambda: what(j, p))
+        for j in range(CHUNKS):
+            p = 2 * j if j < 16 else (1, 17)[j - 16]
+            pl.when(p != q)(functools.partial(what, j, p))
 
     chunks(lambda j, p: scatter(j, q, p).start())
 

time: 62.6 us -> 62 us (level)
  no operation moved by 1% of the time
where the time goes in v3:
time: 62 us; the launch traced here: 61.8 us
  Pallas kernels  57.1 us (92%)
  local copies, waits for them, and re-layouts  4 us (6%)
  between operations  0.65 us (1%)
    pallas_call x1, Pallas kernels, shards(): pl.pallas_call(kernel, out_shape=(jax.ShapeDtypeStruct((C, LANES), BF16),...  57.1 us
    unnamed x5, local copies, waits for them, and re-layouts  4 us

profile of v3, /device:TPU:1, one launch (start us, length us, event | category | flops | bytes accessed | tf_op | source)
XLA Modules:
  0.0 61.8 jit_solution(17840183900486786697)
XLA Ops:
  0.6 57.1 %shard_map.67 = (bf16[320,128]{1,0:T(8,128)(2,1)}, bf16[320,128]{1,0:T(8,128)(2,1)}, f32[864,40]{1,0:T(8,128)}) custom-call(bf16[320,128]{1,0:T(8,128)(2,1)} %bitcast.16, bf16[320,128]{1,0:T(8,128)(2,1)} %bitcast.17, bf16[1536,128]{1,0:T(8,128)(2,1)} %bitcast.14, bf16[3,288,40]{2,1,0:T(8,128)(2,1)} %bitcast.15), custom_call_target="tpu_custom_call" | custom-call | flops 1000000000 | bytes 4000000 | tf_op jit(solution)/shard_map/pallas_call | solution.py:384
  57.7 0.0 copy-start
  57.7 1.6 %copy.10 = bf16[320,1,128]{2,0,1:T(8,128)(2,1)} copy(bf16[320,1,128]{2,0,1:T(8,128)(2,1)} %bitcast.13) | data formatting | bytes 163840
  59.3 0.0 copy-done
  59.3 0.6 %copy.11 = bf16[320,1,128]{2,0,1:T(8,128)(2,1)} copy(bf16[320,1,128]{2,0,1:T(8,128)(2,1)S(1)} %bitcast.12) | data formatting | bytes 163840
  59.9 1.8 %copy.12 = f32[32,40,3,3,3]{1,0,4,3,2:T(8,128)} copy(f32[32,40,3,3,3]{1,0,4,3,2:T(8,128)} %bitcast.11) | data formatting | bytes 276480
Async XLA Ops:
  57.7 1.6 %copy-start = (bf16[320,128]{1,0:T(8,128)(2,1)S(1)}, bf16[320,128]{1,0:T(8,128)(2,1)}, u32[]{:S(2)}) copy-start(bf16[320,128]{1,0:T(8,128)(2,1)} %get-tuple-element.7) | copy-start | bytes 245764
